TPU v7x, 256 devices: a whole 4x4x8 slice. The times are simulated.
256 devices in a mesh: dp: 4 (over y_lo, core), expert: 8 (over z), tensor: 8 (over x, y_hi).
Axes of the slice: x: 4, y: 4 (y_hi: 2, y_lo: 2; y = y_hi * 2 + y_lo), z: 8, core: 2. Of those that a mesh axis runs over, the one named last changes fastest.
Arguments:
- grad_out: bfloat16 [32768, 2048], P(('dp', 'expert', 'tensor')), may hold values from -6 to 6
- expert_ids: int32 [32768, 2], P(('dp', 'expert', 'tensor')), may hold values from 0 to 63, all different within a row; in each aligned block of 128 rows (0 to 127, 128 to 255, ...) at most 5 rows name the same one
- gate_weights: float32 [32768, 2], P(('dp', 'expert', 'tensor')), may hold values from 0.05 to 0.6
- overflow: int32 [32768, 2], P(('dp', 'expert', 'tensor')), may hold values 0 or 1
- saved_gate: bfloat16 [64, 4, 64, 5, 1408], P(('expert', 'tensor'), None, None, None, 'dp'), may hold values from -6 to 6
- saved_up: bfloat16 [64, 4, 64, 5, 1408], P(('expert', 'tensor'), None, None, None, 'dp'), may hold values from -6 to 6
- w_gate: bfloat16 [64, 2048, 1408], P(('expert', 'tensor'), None, 'dp'), may hold values from -0.125 to 0.125
- w_up: bfloat16 [64, 2048, 1408], P(('expert', 'tensor'), None, 'dp'), may hold values from -0.125 to 0.125
- w_down: bfloat16 [64, 1408, 2048], P(('expert', 'tensor'), 'dp'), may hold values from -0.15625 to 0.15625
- shared_gate_act: bfloat16 [32768, 1408], P(('dp', 'expert'), 'tensor'), may hold values from -6 to 6
- shared_up_act: bfloat16 [32768, 1408], P(('dp', 'expert'), 'tensor'), may hold values from -6 to 6
- ws_gate: bfloat16 [2048, 1408], P(None, 'tensor'), may hold values from -0.125 to 0.125
- ws_up: bfloat16 [2048, 1408], P(None, 'tensor'), may hold values from -0.125 to 0.125
- ws_down: bfloat16 [1408, 2048], P('tensor'), may hold values from -0.15625 to 0.15625
- w_out: bfloat16 [2048, 2048], P('tensor'), may hold values from -0.125 to 0.125
Outputs:
- grad_hidden: bfloat16 [32768, 2048], P(('dp', 'expert', 'tensor'))
- grad_context: bfloat16 [32768, 2048], P(('dp', 'expert'), 'tensor')
Inputs may be any that keep to these rules, and one draw needn't show every extreme that they name: `expert_ids`: each row names 2 different experts; within the rows of one device (aligned blocks of 128 rows) no expert is named by more than 5 rows, a bound that some block reaches.
All inputs are finite; a program needn't handle non-finite values. No bound on the sum of `overflow` on one device may be relied on, other than what follows from the above.
Results may differ from a plain program's by a relative error of at most 0.015.
Values may be sent and summed in bfloat16 or wider, within the bound.
A program may use at most 128 MiB of HBM per device.

v0:
```python
import jax
import jax.numpy as jnp
from jax import lax
from jax.sharding import PartitionSpec as P


def rank_in_block(pair_experts, expert_total):
    onehot = (pair_experts[:, None] == jnp.arange(expert_total, dtype=jnp.int32)[None, :]).astype(
        jnp.int32
    )
    earlier = jnp.cumsum(onehot, axis=0) - onehot
    return jnp.sum(earlier * onehot, axis=1)


def fill_slots(pair_grads, pair_experts, expert_total, capacity):
    pair_count, model_width = pair_grads.shape
    destination = pair_experts * capacity + rank_in_block(pair_experts, expert_total)
    source = jnp.full((expert_total * capacity,), pair_count, jnp.int32)
    source = source.at[destination].set(jnp.arange(pair_count, dtype=jnp.int32))
    padded = jnp.concatenate([pair_grads, jnp.zeros((1, model_width), pair_grads.dtype)], axis=0)
    return (padded[source].reshape(expert_total, capacity, model_width), destination)


def weighted_pairs(grads, weights):
    scaled = grads.astype(jnp.float32)[:, None, :] * weights.astype(jnp.float32)[:, :, None]
    return scaled.astype(jnp.bfloat16).reshape(-1, grads.shape[1])


def swiglu_backward(hidden_activation, gate_act, up_act):
    gate_value = gate_act.astype(jnp.float32)
    sigmoid_value = jax.nn.sigmoid(gate_value)
    gate_input_gradient = (
        hidden_activation
        * up_act.astype(jnp.float32)
        * sigmoid_value
        * (1.0 + gate_value * (1.0 - sigmoid_value))
    ).astype(jnp.bfloat16)
    up_input_gradient = (hidden_activation * gate_value * sigmoid_value).astype(jnp.bfloat16)
    return (gate_input_gradient, up_input_gradient)


def expert_terms(
    capacity_slot_rows,
    gate_act,
    up_act,
    gate_projection_weight,
    up_projection_weight,
    down_projection_weight,
):
    hidden_activation = jnp.einsum(
        "cyg,cog->cyo",
        capacity_slot_rows,
        down_projection_weight,
        preferred_element_type=jnp.float32,
    )
    gate_input_gradient, up_input_gradient = swiglu_backward(hidden_activation, gate_act, up_act)
    input_gradient_output = jnp.einsum(
        "etv,ebv->etb",
        gate_input_gradient,
        gate_projection_weight,
        preferred_element_type=jnp.float32,
    )
    input_gradient_output = input_gradient_output + jnp.einsum(
        "etv,ebv->etb", up_input_gradient, up_projection_weight, preferred_element_type=jnp.float32
    )
    return lax.optimization_barrier(input_gradient_output.astype(jnp.bfloat16))


def body(
    grad_out,
    expert_ids,
    gate_weights,
    overflow,
    saved_gate,
    saved_up,
    w_gate,
    w_up,
    w_down,
    shared_gate_act,
    shared_up_act,
    ws_gate,
    ws_up,
    ws_down,
    w_out,
):
    dp_count = lax.axis_size("dp")
    group_count = lax.axis_size(("expert", "tensor"))
    expert_local, unused_dp, unused_group, capacity, unit_part = saved_gate.shape
    expert_total = expert_local * group_count
    token_count, model_width = grad_out.shape
    top_count = expert_ids.shape[1]
    flag_values = overflow.astype(jnp.float32)
    routed_weight = (gate_weights * (1.0 - flag_values)).astype(jnp.bfloat16)
    shared_weight = 1.0 + jnp.sum(gate_weights * flag_values, axis=1)
    pair_grads = weighted_pairs(grad_out, routed_weight)
    filled, destination = fill_slots(pair_grads, expert_ids.reshape(-1), expert_total, capacity)
    arrived = lax.all_to_all(
        filled[:, None], ("expert", "tensor"), split_axis=0, concat_axis=1, tiled=True
    )
    everyone = lax.all_gather(arrived[:, None], "dp", axis=1, tiled=True)
    terms = expert_terms(
        everyone.reshape(expert_local, -1, model_width),
        saved_gate.reshape(expert_local, -1, unit_part),
        saved_up.reshape(expert_local, -1, unit_part),
        w_gate,
        w_up,
        w_down,
    )
    terms = terms.astype(jnp.float32).reshape(
        expert_local, dp_count, group_count, capacity, model_width
    )
    summed = lax.psum_scatter(
        terms.astype(jnp.bfloat16), "dp", scatter_dimension=1, tiled=True
    ).astype(jnp.float32)
    returned = lax.all_to_all(
        summed[:, 0].astype(jnp.bfloat16),
        ("expert", "tensor"),
        split_axis=1,
        concat_axis=0,
        tiled=True,
    ).astype(jnp.float32)
    picked = returned.reshape(expert_total * capacity, model_width)[destination]
    routed = jnp.sum(picked.reshape(token_count, top_count, model_width), axis=1)
    routed_total = routed.astype(jnp.bfloat16)
    shared_grad = (grad_out.astype(jnp.float32) * shared_weight[:, None]).astype(jnp.bfloat16)
    group_shared = lax.all_gather(shared_grad, "tensor", axis=0, tiled=True)
    shared_hidden = jnp.einsum(
        "td,fd->tf", group_shared, ws_down, preferred_element_type=jnp.float32
    )
    shared_gate_grad, shared_up_grad = swiglu_backward(
        shared_hidden, shared_gate_act, shared_up_act
    )
    partial_value = jnp.einsum(
        "tf,df->td", shared_gate_grad, ws_gate, preferred_element_type=jnp.float32
    )
    partial_value = partial_value + jnp.einsum(
        "tf,df->td", shared_up_grad, ws_up, preferred_element_type=jnp.float32
    )
    partial_value = lax.optimization_barrier(partial_value.astype(jnp.bfloat16)).astype(jnp.float32)
    shared_total = lax.psum(partial_value.astype(jnp.bfloat16), "tensor").astype(jnp.float32)
    group_grads, group_routed = (
        lax.all_gather(grad_out, "tensor", axis=0, tiled=True),
        lax.all_gather(routed_total, "tensor", axis=0, tiled=True),
    )
    grad_group = (
        group_grads.astype(jnp.float32) + shared_total + group_routed.astype(jnp.float32)
    ).astype(jnp.bfloat16)
    position = lax.axis_index("tensor") * token_count
    grad_hidden = lax.dynamic_slice_in_dim(grad_group, position, token_count, 0)
    grad_context = jnp.einsum(
        "td,hd->th", grad_group, w_out, preferred_element_type=jnp.float32
    ).astype(jnp.bfloat16)
    return (grad_hidden, grad_context)


def solution(mesh):
    in_specs = (
        P(("dp", "expert", "tensor"), None),
        P(("dp", "expert", "tensor"), None),
        P(("dp", "expert", "tensor"), None),
        P(("dp", "expert", "tensor"), None),
        P(("expert", "tensor"), None, None, None, "dp"),
        P(("expert", "tensor"), None, None, None, "dp"),
        P(("expert", "tensor"), None, "dp"),
        P(("expert", "tensor"), None, "dp"),
        P(("expert", "tensor"), "dp", None),
        P(("dp", "expert"), "tensor"),
        P(("dp", "expert"), "tensor"),
        P(None, "tensor"),
        P(None, "tensor"),
        P("tensor", None),
        P("tensor", None),
    )
    out_specs = (P(("dp", "expert", "tensor"), None), P(("dp", "expert"), "tensor"))
    return jax.shard_map(body, mesh=mesh, in_specs=in_specs, out_specs=out_specs, check_vma=False)
```

profile of v0, /device:TPU:24, one launch (start us, length us, event | category | flops | bytes accessed | tf_op | source)
XLA Modules:
  0.0 689.0 jit_solution(10206642360038884631)
XLA Ops:
  7.2 0.0 all-gather.12.cloned.1.call-start
  7.2 0.9 copy.32
  8.1 0.1 eq.29
  8.3 0.1 eq.25
  8.4 0.7 broadcast_multiply_fusion
  9.1 0.6 reduce-window.6
  9.7 0.2 slice_reduce_fusion
  9.9 0.1 copy.31
  10.1 0.1 mul.116
  10.2 0.1 fusion.23
  10.3 1.4 scatter_custom_fusion
  11.7 0.7 multiply_reduce_fusion
  12.5 0.1 copy.30
  12.6 0.1 reshape.157
  12.7 2.1 mul.107
  14.8 2.5 mul.108
  17.3 1.8 multiply_convert_fusion
  19.1 0.1 concatenate.3
  19.2 3.0 gather_fusion
  22.2 2.4 broadcast_in_dim_reshape.4
  24.6 64.6 %all_to_all.8 = bf16[64,1,5,2048]{3,2,1,0:T(8,128)(2,1)S(1)} all-to-all(bf16[64,1,5,2048]{3,2,1,0:T(8,128)(2,1)S(1)} %bitcast.47), channel_id=1, replica_groups=mesh['dp'=4,'expert'=8,'tensor'=8] {'expert','tensor'}, dimensions={0} | all-to-all | bytes 2621440 | tf_op jit(solution)/shard_map/all_to_all | solution.py:97
  89.2 2.0 copy.36
  91.2 0.0 all-gather.12.cloned.1.call-update
  91.2 0.0 all-gather.8.cloned.1.call-start
  91.3 0.9 multiply_convert_fusion.3
  92.2 0.0 all-gather.8.cloned.1.call-update
  92.3 0.0 reduce-scatter.2.cloned.1.call-start
  92.3 0.2 copy-done.6
  92.5 2.3 copy.40
  94.7 3.6 reshape.159
  98.3 2.0 copy.41
  100.4 3.6 copy.38
  104.0 3.6 reshape.158
  107.6 2.8 copy.39
  110.4 34.1 %all-gather.12.cloned.1.call-done = bf16[256,1,5,2048]{3,0,2,1:T(8,128)(2,1)} async-done(((bf16[64,1,5,2048]{3,0,2,1:T(8,128)(2,1)}), bf16[256,1,5,2048]{3,0,2,1:T(8,128)(2,1)}) %all-gather.12.cloned.1.call-update) | async-done | bytes 5242896 | tf_op jit(solution)/shard_map/all_gather | solution.py:100
  144.5 8.9 %copy.37 = bf16[256,1,5,2048]{3,2,0,1:T(8,128)(2,1)} copy(bf16[256,1,5,2048]{3,0,2,1:T(8,128)(2,1)} %all-gather.12.cloned.1.call-done) | data formatting | bytes 10485760 | tf_op jit(solution)/shard_map/all_gather | solution.py:100
  153.4 10.1 %reshape.152 = bf16[1280,2048]{1,0:T(8,128)(2,1)} reshape(bf16[256,1,5,2048]{3,2,0,1:T(8,128)(2,1)} %copy.37) | data formatting | bytes 10485760 | tf_op jit(solution)/shard_map/reshape.6
  163.5 5.1 fusion.4
  168.7 3.3 fusion.2
  172.0 5.0 fusion
  177.0 9.8 %convert_element_type.145 = bf16[1,4,64,5,2048]{4,3,2,1,0:T(8,128)(2,1)} reshape(bf16[1,1280,2048]{2,1,0:T(8,128)(2,1)} %fusion) | data formatting | bytes 10485760 | tf_op jit(solution)/shard_map/convert_element_type | solution.py:113
  186.8 0.0 reduce-scatter.2.cloned.1.call-update
  186.8 0.0 all-gather.6.cloned.1.call-start
  186.9 0.5 all-gather.6.cloned.1.call-update
  187.4 0.0 all-reduce.3.cloned.1.call-start
  187.5 37.6 %all-gather.8.cloned.1.call-done = bf16[1024,2048]{1,0:T(8,128)(2,1)} async-done(((bf16[128,2048]{1,0:T(8,128)(2,1)}), bf16[1024,2048]{1,0:T(8,128)(2,1)}) %all-gather.8.cloned.1.call-update) | async-done | bytes 4194320 | tf_op jit(solution)/shard_map/all_gather | solution.py:126
  225.1 3.7 fusion.32
  228.8 1.4 fusion.17
  230.3 3.3 add_convert_fusion.2
  233.6 74.6 %reduce-scatter.2.cloned.1.call-done = bf16[1,1,64,5,2048]{4,3,2,1,0:T(8,128)(2,1)} async-done(((bf16[1,4,64,5,2048]{4,3,2,1,0:T(8,128)(2,1)}), bf16[1,1,64,5,2048]{4,3,2,1,0:T(8,128)(2,1)}) %reduce-scatter.2.cloned.1.call-update) | async-done | bytes 1310736 | tf_op jit(solution)/shard_map/reduce_scatter | solution.py:112
  308.2 13.2 %all-to-all-start.1 = ((bf16[1,64,5,2048]{3,2,0,1:T(8,128)(2,1)}), bf16[1,64,5,2048]{3,2,0,1:T(8,128)(2,1)}, u32[]{:S(2)}, u32[]{:S(2)}) async-start(bf16[1,64,5,2048]{3,2,0,1:T(8,128)(2,1)} %bitcast.48), calls=%async_computation.2 | async-start | bytes 4194304 | tf_op jit(solution)/shard_map/all_to_all | solution.py:115
  321.4 0.0 all-gather.10.cloned.1.call-start
  321.4 50.5 %all-to-all-done.1 = bf16[1,64,5,2048]{3,2,0,1:T(8,128)(2,1)} async-done(((bf16[1,64,5,2048]{3,2,0,1:T(8,128)(2,1)}), bf16[1,64,5,2048]{3,2,0,1:T(8,128)(2,1)}, u32[]{:S(2)}, u32[]{:S(2)}) %all-to-all-start.1) | async-done | bytes 1310752 | tf_op jit(solution)/shard_map/all_to_all | solution.py:115
  371.9 2.5 reshape.160
  374.5 2.7 gather_fusion.1
  377.2 2.5 reshape.156
  379.7 3.8 reduce_sum.32
  383.4 0.0 all-gather.10.cloned.1.call-update
  383.5 16.2 %all-gather.6.cloned.1.call-done = bf16[1024,2048]{1,0:T(8,128)(2,1)} async-done(((bf16[128,2048]{1,0:T(8,128)(2,1)}), bf16[1024,2048]{1,0:T(8,128)(2,1)}) %all-gather.6.cloned.1.call-update) | async-done | bytes 4194320 | tf_op jit(solution)/shard_map/all_gather | solution.py:142
  399.7 190.4 %all-reduce.3.cloned.1.call-done = bf16[1024,2048]{1,0:T(8,128)(2,1)} async-done(((bf16[1024,2048]{1,0:T(8,128)(2,1)}), bf16[1024,2048]{1,0:T(8,128)(2,1)}) %all-reduce.3.cloned.1.call-update) | async-done | bytes 4194320 | tf_op jit(solution)/shard_map/psum | solution.py:140
  590.1 81.5 %all-gather.10.cloned.1.call-done = bf16[1024,2048]{1,0:T(8,128)(2,1)} async-done(((bf16[128,2048]{1,0:T(8,128)(2,1)}), bf16[1024,2048]{1,0:T(8,128)(2,1)}) %all-gather.10.cloned.1.call-update) | async-done | bytes 4194320 | tf_op jit(solution)/shard_map/all_gather | solution.py:143
  671.6 7.6 %add_convert_fusion.1 = bf16[1024,2048]{1,0:T(8,128)(2,1)S(1)} fusion(bf16[1024,2048]{1,0:T(8,128)(2,1)} %all-gather.10.cloned.1.call-done, bf16[1024,2048]{1,0:T(8,128)(2,1)} %all-reduce.3.cloned.1.call-done, bf16[1024,2048]{1,0:T(8,128)(2,1)} %all-gather.6.cloned.1.call-done), kind=kLoop, calls=%fused_computation.4 | loop fusion | flops 12582912 | bytes 16777216 | tf_op jit(solution)/shard_map/convert_element_type | solution.py:147
  679.2 0.8 constant_dynamic-slice_fusion
  680.0 2.1 convolution_convert_fusion
  (33 shorter events, 0.2 us)
Async XLA Ops:
  7.2 161.5 %copy-start = (bf16[1,2048,352]{1,2,0:T(8,128)(2,1)S(1)}, bf16[1,2048,352]{1,2,0:T(8,128)(2,1)}, u32[]{:S(2)}) copy-start(bf16[1,2048,352]{1,2,0:T(8,128)(2,1)} %param.21) | copy-start | bytes 4325380
  7.2 137.3 %all-gather.12.cloned.1.call-start = ((), (), s32[]{:S(2)}) async-start(), calls=%async_computation.8 | async-start | bytes 6553600 | tf_op jit(solution)/shard_map/all_gather | solution.py:100
  89.2 2.0 copy-start.3
  91.2 1.3 copy-start.6
  91.2 133.9 %all-gather.8.cloned.1.call-start = ((), (), s32[]{:S(2)}) async-start(), calls=%async_computation.4 | async-start | bytes 4718592 | tf_op jit(solution)/shard_map/all_gather | solution.py:126
  92.3 216.0 %reduce-scatter.2.cloned.1.call-start = ((), (), s32[]{:S(2)}) async-start(), calls=%async_computation.6 | async-start | bytes 10485760 | tf_op jit(solution)/shard_map/reduce_scatter | solution.py:112
  163.5 5.2 copy-start.2
  168.7 3.3 copy-start.5
  186.8 38.3 %copy-start.11 = (bf16[176,2048]{1,0:T(8,128)(2,1)S(1)}, bf16[176,2048]{1,0:T(8,128)(2,1)}, u32[]{:S(2)}) copy-start(bf16[176,2048]{1,0:T(8,128)(2,1)} %param.28) | copy-start | bytes 2162692
  186.8 212.9 %all-gather.6.cloned.1.call-start = ((), (), s32[]{:S(2)}) async-start(), calls=%async_computation.3 | async-start | bytes 4718592 | tf_op jit(solution)/shard_map/all_gather | solution.py:142
  187.4 41.4 %copy-start.4 = (bf16[1024,176]{0,1:T(8,128)(2,1)S(1)}, bf16[1024,176]{0,1:T(8,128)(2,1)}, u32[]{:S(2)}) copy-start(bf16[1024,176]{0,1:T(8,128)(2,1)} %param.24) | copy-start | bytes 1081348
  187.4 41.4 %copy-start.8 = (bf16[2048,176]{0,1:T(8,128)(2,1)S(1)}, bf16[2048,176]{0,1:T(8,128)(2,1)}, u32[]{:S(2)}) copy-start(bf16[2048,176]{0,1:T(8,128)(2,1)} %param.26) | copy-start | bytes 2162692
  187.4 41.4 %copy-start.9 = (bf16[1024,176]{0,1:T(8,128)(2,1)S(1)}, bf16[1024,176]{0,1:T(8,128)(2,1)}, u32[]{:S(2)}) copy-start(bf16[1024,176]{0,1:T(8,128)(2,1)} %param.25) | copy-start | bytes 1081348
  187.4 402.7 %all-reduce.3.cloned.1.call-start = ((), (), s32[]{:S(2)}) async-start(), calls=%async_computation.5 | async-start | bytes 8388608 | tf_op jit(solution)/shard_map/psum | solution.py:140
  228.8 1.4 copy-start.7
  308.2 63.7 %all-to-all-start.1 = ((bf16[1,64,5,2048]{3,2,0,1:T(8,128)(2,1)}), bf16[1,64,5,2048]{3,2,0,1:T(8,128)(2,1)}, u32[]{:S(2)}, u32[]{:S(2)}) async-start(bf16[1,64,5,2048]{3,2,0,1:T(8,128)(2,1)} %bitcast.48), calls=%async_computation.2 | async-start | bytes 4194304 | tf_op jit(solution)/shard_map/all_to_all | solution.py:115
  321.4 350.2 %all-gather.10.cloned.1.call-start = ((), (), s32[]{:S(2)}) async-start(), calls=%async_computation.7 | async-start | bytes 4718592 | tf_op jit(solution)/shard_map/all_gather | solution.py:143
  383.5 296.6 %copy-start.10 = (bf16[256,2048]{1,0:T(8,128)(2,1)S(1)}, bf16[256,2048]{1,0:T(8,128)(2,1)}, u32[]{:S(2)}) copy-start(bf16[256,2048]{1,0:T(8,128)(2,1)} %param.29) | copy-start | bytes 3145732
  680.0 2.1 copy-start.1
Sparse Core Ops, SparseCore 0:
  91.3 53.1 all-gather.11
  147.7 77.3 all-gather.7
  227.7 80.4 reduce-scatter.1
  310.7 88.9 all-gather.5
  402.2 187.8 all-reduce.2
  593.2 78.3 all-gather.9
where the time goes:
time: 693 us; the launch traced here: 689 us
  waiting for transfers between devices  486 us (70%)
  local copies, waits for them, and re-layouts  70.7 us (10%)
  blocking collectives  64.6 us (9%)
  matrix products  24 us (3%)
  other arithmetic  16.3 us (2%)
  between operations  14.4 us (2%)
  starting transfers between devices  13.4 us (2%)
    psum x1, waiting for transfers between devices, body(): lax.psum(partial_value.astype(jnp.bfloat16), 'tensor').astype(jnp.float32)  190 us
    all_gather x1, waiting for transfers between devices, body(): lax.all_gather(routed_total, 'tensor', axis=0, tiled=True)  81.5 us
    reduce_scatter x1, waiting for transfers between devices, body(): lax.psum_scatter(terms.astype(jnp.bfloat16), 'dp', scatter_dimension=1, t...  74.6 us
    all_to_all x1, blocking collectives, body(): lax.all_to_all(filled[:, None], ('expert', 'tensor'), split_axis=0, conca...  64.6 us
    all_to_all x1, waiting for transfers between devices, body(): lax.all_to_all(summed[:, 0].astype(jnp.bfloat16), ('expert', 'tensor'), s...  50.5 us
    all_gather x1, waiting for transfers between devices, body(): group_shared = lax.all_gather(shared_grad, 'tensor', axis=0, tiled=True)  37.6 us
    all_gather x1, waiting for transfers between devices, body(): everyone = lax.all_gather(arrived[:, None], 'dp', axis=1, tiled=True)  34.1 us
    all_gather x1, waiting for transfers between devices, body(): lax.all_gather(grad_out, 'tensor', axis=0, tiled=True)  16.2 us
  transfers between devices with their start and end apart: 7, of which 7 were waited for; matrix products, arithmetic and copies ran while one was open for 12% of the time, Pallas kernels for 0%

commit v1 on v0

v1 whole, which is shorter than its diff:
```python
import functools

import jax
import jax.numpy as jnp
from jax import lax
from jax.experimental import pallas as pl
from jax.experimental.pallas import tpu as pltpu
from jax.sharding import PartitionSpec as P

MESH = pl.DeviceIdType.MESH
BF = jnp.bfloat16
F32 = jnp.float32
CHUNKS = 2
TOK = 128
D = 2048
WIDTH = D // CHUNKS
CAP = 5
PLANE = CAP * 8
ROWS = 8 * PLANE
FE = 352
FS = 176
DEPTH = 768
N_SEM = 160


def nn(a, b):
    return jnp.dot(a, b, preferred_element_type=F32)


def nt(a, b):
    return lax.dot_general(a, b, (((1,), (1,)), ((), ())), preferred_element_type=F32)


def swiglu_backward(hidden, gate_act, up_act):
    s = jax.nn.sigmoid(gate_act)
    gate = hidden * up_act * s * (1.0 + gate_act * (1.0 - s))
    up = hidden * gate_act * s
    return gate, up


def rows_of(planes):
    return planes.astype(F32).reshape(ROWS, planes.shape[-1])


def kernel(
    grad_ref, ids_ref, gw_ref, ov_ref, sgate_hbm, sup_hbm, wg_hbm, wu_hbm, wd_hbm,
    shg_hbm, shu_hbm, wsg_hbm, wsu_hbm, wsd_hbm, wo_hbm,
    hid_out, ctx_out,
    G, info, zs, A, Ts, Tr, Us, Ur, V, Z, far_s, near_s, y_s, far_r, near_r, y_r, H,
    wd, wgu, wsd, wo, sgate, sup, shg, shu, hid, gu, Pm, Wr, Lf, LT, Rk, own, ctx,
    ss, rs, ls,
):
    dp, z, t = lax.axis_index("dp"), lax.axis_index("expert"), lax.axis_index("tensor")
    ylo, core, x, yh = dp // 2, dp % 2, t // 2, t % 2
    xr, xl, xf = (x + 1) % 4, (x + 3) % 4, (x + 2) % 4
    yo = 1 - yh
    right, left, across = (dp, z, xr * 2 + yh), (dp, z, xl * 2 + yh), (dp, z, x * 2 + yo)
    sib = (ylo * 2 + 1 - core, z, t)
    opp = ((1 - ylo) * 2 + core, z, t)
    sib_dp, opp_dp, dia_dp = ylo * 2 + 1 - core, (1 - ylo) * 2 + core, (1 - ylo) * 2 + 1 - core

    count = [0]
    sent = []

    def send(src, dst, dev):
        i = count[0]
        count[0] += 1
        cp = pltpu.make_async_remote_copy(
            src_ref=src, dst_ref=dst, send_sem=ss.at[i], recv_sem=rs.at[i],
            device_id=dev, device_id_type=MESH,
        )
        cp.start()
        sent.append(cp)
        return cp

    locals_ = [0]

    def fetch(src, dst):
        i = locals_[0]
        locals_[0] += 1
        cp = pltpu.make_async_copy(src, dst, ls.at[i])
        cp.start()
        return cp

    tens = [(dx, dy) for dx in range(4) for dy in range(2) if dx or dy]

    own_in = [fetch(grad_ref.at[:, pl.ds(c * WIDTH, WIDTH)], G.at[c, t]) for c in range(CHUNKS)]
    barrier = pltpu.get_barrier_semaphore()
    peers = [(dp, z, ((x + dx) % 4) * 2 + (yh + dy) % 2) for dx, dy in tens]
    peers += [(dp, (z + dz) % 8, t) for dz in range(1, 8)]
    peers += [sib, opp]
    for p in peers:
        pl.semaphore_signal(barrier, inc=1, device_id=p, device_id_type=MESH)

    pend = dict(
        wd=fetch(wd_hbm, wd),
        wsd=fetch(wsd_hbm, wsd),
        wg=fetch(wg_hbm, wgu.at[pl.ds(0, FE)]),
        wu=fetch(wu_hbm, wgu.at[pl.ds(384, FE)]),
        wo=fetch(wo_hbm, wo),
        sgate=fetch(sgate_hbm, sgate),
        sup=fetch(sup_hbm, sup),
        shg=fetch(shg_hbm, shg),
        shu=fetch(shu_hbm, shu),
    )
    ws_in = []
    for c in range(CHUNKS):
        cols = pl.ds(c * WIDTH, WIDTH)
        ws_in.append(fetch(wsg_hbm.at[:, cols], Rk.at[c, pl.ds(ROWS, FS)]))
        ws_in.append(fetch(wsu_hbm.at[:, cols], Rk.at[c, pl.ds(ROWS + FS, FS)]))

    ids = ids_ref[...]
    gw = gw_ref[...]
    ov = ov_ref[...].astype(F32)
    experts = lax.broadcasted_iota(jnp.int32, (64, TOK), 0)
    oh = [(experts == ids[k : k + 1, :]).astype(F32) for k in range(2)]
    upper = lax.broadcasted_iota(jnp.int32, (TOK, TOK), 0) < lax.broadcasted_iota(
        jnp.int32, (TOK, TOK), 1
    )
    earlier = nn((oh[0] + oh[1]).astype(BF), upper.astype(F32).astype(BF))
    slots = [jnp.sum(earlier * oh[k], axis=0, keepdims=True) for k in range(2)]
    routed_weight = (gw * (1.0 - ov)).astype(BF).astype(F32)
    shared_weight = 1.0 + jnp.sum(gw * ov, axis=0, keepdims=True)
    info[t] = jnp.concatenate(
        [ids.astype(F32), slots[0], slots[1], routed_weight, shared_weight, shared_weight], axis=0
    )

    pl.semaphore_wait(barrier, len(peers))

    def gather0(buf, c):
        src = buf.at[c, t]
        return dict(
            y=send(src, src, across), r=send(src, src, right), l=send(src, src, left)
        )

    def gather1(buf, c, st):
        st["y"].wait_recv()
        src = buf.at[c, x * 2 + yo]
        st["pr"] = send(src, src, right)
        st["pl"] = send(src, src, left)

    def forward(buf, c, st, half):
        a = buf.at[c, xl * 2 + half, pl.ds(0, TOK // 2)]
        b = buf.at[c, xr * 2 + half, pl.ds(TOK // 2, TOK // 2)]
        st.setdefault("far", []).extend([send(a, a, right), send(b, b, left)])

    def gather2(buf, c, st):
        st["r"].wait_recv()
        st["l"].wait_recv()
        forward(buf, c, st, yh)

    def gather3(buf, c, st):
        st["pr"].wait_recv()
        st["pl"].wait_recv()
        forward(buf, c, st, yo)

    def gather4(buf, c, st):
        for cp in st["far"]:
            cp.wait_recv()

    def gather_all(buf):
        st = []
        for c in range(CHUNKS):
            st.append(gather0(buf, c))
        return st

    st = []
    own_in[0].wait()
    st.append(gather0(G, 0))
    infos = [send(info.at[t], info.at[t], p) for p in peers[: len(tens)]]
    for c in range(1, CHUNKS):
        own_in[c].wait()

    for cp in infos:
        cp.wait_recv()
    row_ids = lax.broadcasted_iota(jnp.int32, (ROWS, TOK), 0)
    weight = jnp.zeros((ROWS, 1), F32)
    Lf[...] = jnp.zeros_like(Lf)
    for b in range(8):
        part = info[b]
        hit = []
        for k in range(2):
            e = part[k : k + 1, :].astype(jnp.int32)
            j = part[2 + k : 3 + k, :].astype(jnp.int32)
            code = jnp.where(e % 8 == t, (e // 8) * PLANE + j * 8 + b, -1)
            on = (row_ids == code).astype(F32)
            weight = weight + jnp.sum(on * part[4 + k : 5 + k, :], axis=1, keepdims=True)
            hit.append(on)
        both = hit[0] + hit[1]
        Lf[0:ROWS, b * TOK : (b + 1) * TOK] = both
        Pm[:, b * TOK : (b + 1) * TOK] = both.astype(BF)
    Wr[...] = jnp.broadcast_to(weight, Wr.shape)

    def dispatch(c):
        got = nn(Pm[...], G[c].reshape(8 * TOK, WIDTH)) * Wr[:, 0:1]
        zs[c] = got.reshape(8, PLANE, WIDTH).astype(BF)
        A[c, dp, z] = zs[c, z]
        return [
            send(zs.at[c, (z + dz) % 8], A.at[c, dp, z], (dp, (z + dz) % 8, t))
            for dz in (1, 7, 2, 6, 3, 5, 4)
        ]

    gather1(G, 0, st[0])
    gather2(G, 0, st[0])
    for c in range(1, CHUNKS):
        st.append(gather0(G, c))
        gather3(G, c - 1, st[c - 1])
        gather1(G, c, st[c])
        gather4(G, c - 1, st[c - 1])
        if c == 1:
            zin = []
        zin.append(dispatch(c - 1))
        gather2(G, c, st[c])
    last = CHUNKS - 1
    gather3(G, last, st[last])
    gather4(G, last, st[last])
    zin.append(dispatch(last))

    pend["wsd"].wait()
    pend["shg"].wait()
    pend["shu"].wait()
    sw = jnp.concatenate([info[b, 6:7, :] for b in range(8)], axis=1)
    sh = jnp.zeros((FS, 8 * TOK), F32)
    for c in range(CHUNKS):
        sh = sh + nt(wsd[:, c * WIDTH : (c + 1) * WIDTH], G[c].reshape(8 * TOK, WIDTH))
    sg, su = swiglu_backward(sh * sw, shg[...].astype(F32), shu[...].astype(F32))
    Lf[ROWS : ROWS + FS, :] = sg
    Lf[ROWS + FS : ROWS + 2 * FS, :] = su
    for b in range(8):
        LT[b] = jnp.transpose(Lf[:, b * TOK : (b + 1) * TOK]).astype(BF)

    pend["wd"].wait()
    core_in, opp_in = [], []

    def spread(c):
        for cp in zin[c]:
            cp.wait_recv()
        opp_in.append(send(A.at[c, dp], A.at[c, dp], opp))
        core_in.append([send(A.at[c, dp], A.at[c, dp], sib)])

    def spread_on(c):
        opp_in[c].wait_recv()
        core_in[c].append(send(A.at[c, opp_dp], A.at[c, opp_dp], sib))

    def hidden_of(c, d):
        w = wd[:, c * WIDTH : (c + 1) * WIDTH]
        h = nt(rows_of(A[c, d]).astype(BF), w)
        if c == 0:
            hid[d] = h
        else:
            hid[d] = hid[d] + h

    spread(0)
    for c in range(1, CHUNKS):
        hidden_of(c - 1, dp)
        spread_on(c - 1)
        spread(c)
        hidden_of(c - 1, opp_dp)
        for cp in core_in[c - 1]:
            cp.wait_recv()
        hidden_of(c - 1, sib_dp)
        hidden_of(c - 1, dia_dp)
    hidden_of(last, dp)
    spread_on(last)
    pend["sgate"].wait()
    pend["sup"].wait()

    def act(d):
        h4 = hid[d].reshape(8, CAP, 8, FE)
        gs, us = [], []
        for j in range(CAP):
            g, u = swiglu_backward(
                h4[:, j],
                sgate[d, j].astype(F32).reshape(8, 8, FE),
                sup[d, j].astype(F32).reshape(8, 8, FE),
            )
            gs.append(g)
            us.append(u)
        gu[d, :, 0:FE] = jnp.stack(gs, axis=1).reshape(ROWS, FE).astype(BF)
        gu[d, :, 384 : 384 + FE] = jnp.stack(us, axis=1).reshape(ROWS, FE).astype(BF)

    gu[...] = jnp.zeros_like(gu)
    wgu[FE:384, :] = jnp.zeros((384 - FE, D), BF)
    wgu[384 + FE : DEPTH, :] = jnp.zeros((DEPTH - 384 - FE, D), BF)
    hidden_of(last, opp_dp)
    core_in[last][0].wait_recv()
    hidden_of(last, sib_dp)
    act(sib_dp)
    core_in[last][1].wait_recv()
    hidden_of(last, dia_dp)
    act(dia_dp)
    act(opp_dp)
    act(dp)

    pend["wg"].wait()
    pend["wu"].wait()

    def term(c, d):
        return nn(gu[d], wgu[:, c * WIDTH : (c + 1) * WIDTH])

    def planes(v):
        return v.reshape(8, PLANE, WIDTH).astype(BF)

    t_in, u_in, z_back = [], [], []
    for c in range(CHUNKS):
        Ts[c, 0] = planes(term(c, dia_dp))
        a = send(Ts.at[c, 0], Tr.at[c, 0], sib)
        Ts[c, 1] = planes(term(c, sib_dp))
        b = send(Ts.at[c, 1], Tr.at[c, 1], sib)
        t_in.append((a, b))
    for c in range(CHUNKS):
        v = term(c, opp_dp)
        t_in[c][0].wait_recv()
        Us[c] = planes(v + rows_of(Tr[c, 0]))
        u_in.append(send(Us.at[c], Ur.at[c], opp))
    for c in range(CHUNKS):
        v = term(c, dp)
        t_in[c][1].wait_recv()
        v = v + rows_of(Tr[c, 1])
        u_in[c].wait_recv()
        V[c] = planes(v + rows_of(Ur[c]))
        Z[c, z] = V[c, z]
        z_back.append([
            send(V.at[c, (z + dz) % 8], Z.at[c, z], (dp, (z + dz) % 8, t))
            for dz in (1, 7, 2, 6, 3, 5, 4)
        ])
    for cp in ws_in:
        cp.wait()

    def partial(c, place):
        w = LT[pl.ds(place * 2, 2)].reshape(2 * TOK, DEPTH)
        return nn(w, Rk[c]).reshape(2, TOK, WIDTH)

    half = TOK // 2
    fars, nears, ys = [], [], []

    def sum_far(c):
        for cp in z_back[c]:
            cp.wait_recv()
        Rk[c, 0:ROWS] = rows_of(Z[c]).astype(BF)
        Rk[c, ROWS + 2 * FS : DEPTH] = jnp.zeros((DEPTH - ROWS - 2 * FS, WIDTH), BF)
        v = partial(c, xf).astype(BF)
        far_s[c, 0] = v[:, 0:half]
        far_s[c, 1] = v[:, half:TOK]
        fars.append([
            send(far_s.at[c, 0], far_r.at[c, 0], right),
            send(far_s.at[c, 1], far_r.at[c, 1], left),
        ])

    def sum_near(c):
        a = partial(c, xr)
        b = partial(c, xl)
        fars[c][0].wait_recv()
        near_s[c, 0, :, 0:half] = (a[:, 0:half] + far_r[c, 0].astype(F32)).astype(BF)
        near_s[c, 0, :, half:TOK] = a[:, half:TOK].astype(BF)
        r = send(near_s.at[c, 0], near_r.at[c, 0], right)
        fars[c][1].wait_recv()
        near_s[c, 1, :, 0:half] = b[:, 0:half].astype(BF)
        near_s[c, 1, :, half:TOK] = (b[:, half:TOK] + far_r[c, 1].astype(F32)).astype(BF)
        l = send(near_s.at[c, 1], near_r.at[c, 1], left)
        nears.append((r, l))

    def sum_own(c):
        own[...] = partial(c, x)
        nears[c][0].wait_recv()
        nears[c][1].wait_recv()
        y_s[c] = (
            own[yo] + near_r[c, 0, yo].astype(F32) + near_r[c, 1, yo].astype(F32)
        ).astype(BF)
        ys.append(send(y_s.at[c], y_r.at[c], across))
        own[yh] = own[yh] + near_r[c, 0, yh].astype(F32) + near_r[c, 1, yh].astype(F32)

    def finish(c):
        ys[c].wait_recv()
        v = (own[yh] + y_r[c].astype(F32) + G[c, t].astype(F32)).astype(BF)
        H[c, t] = v
        hid_out[:, c * WIDTH : (c + 1) * WIDTH] = v

    hs = []
    sum_far(0)
    for c in range(CHUNKS):
        sum_near(c)
        if c + 1 < CHUNKS:
            sum_far(c + 1)
        sum_own(c)
        finish(c)
        hs.append(gather0(H, c))
    for c in range(CHUNKS):
        gather1(H, c, hs[c])
        gather2(H, c, hs[c])
    pend["wo"].wait()
    for c in range(CHUNKS):
        gather3(H, c, hs[c])
    for c in range(CHUNKS):
        gather4(H, c, hs[c])
        v = nt(H[c].reshape(8 * TOK, WIDTH), wo[:, c * WIDTH : (c + 1) * WIDTH])
        if c == 0:
            ctx[...] = v
        else:
            ctx[...] = ctx[...] + v
    ctx_out[...] = ctx[...].astype(BF)
    for cp in sent:
        cp.wait_send()


def body(
    grad_out, expert_ids, gate_weights, overflow, saved_gate, saved_up, w_gate, w_up, w_down,
    shared_gate_act, shared_up_act, ws_gate, ws_up, ws_down, w_out,
):
    anyspace = pl.BlockSpec(memory_space=pl.ANY)
    vmem = pl.BlockSpec(memory_space=pltpu.VMEM)
    C, W = CHUNKS, WIDTH
    scratch = [
        ((C, 8, TOK, W), BF),
        ((8, 8, TOK), F32),
        ((C, 8, PLANE, W), BF),
        ((C, 4, 8, PLANE, W), BF),
        ((C, 2, 8, PLANE, W), BF),
        ((C, 2, 8, PLANE, W), BF),
        ((C, 8, PLANE, W), BF),
        ((C, 8, PLANE, W), BF),
        ((C, 8, PLANE, W), BF),
        ((C, 8, PLANE, W), BF),
        ((C, 2, 2, TOK // 2, W), BF),
        ((C, 2, 2, TOK, W), BF),
        ((C, TOK, W), BF),
        ((C, 2, 2, TOK // 2, W), BF),
        ((C, 2, 2, TOK, W), BF),
        ((C, TOK, W), BF),
        ((C, 8, TOK, W), BF),
        ((FE, D), BF),
        ((DEPTH, D), BF),
        ((FS, D), BF),
        ((256, D), BF),
        ((4, CAP, 64, FE), BF),
        ((4, CAP, 64, FE), BF),
        ((FS, 8 * TOK), BF),
        ((FS, 8 * TOK), BF),
        ((4, ROWS, FE), F32),
        ((4, ROWS, DEPTH), BF),
        ((ROWS, 8 * TOK), BF),
        ((ROWS, TOK), F32),
        ((DEPTH, 8 * TOK), F32),
        ((8, TOK, DEPTH), BF),
        ((C, DEPTH, W), BF),
        ((2, TOK, W), F32),
        ((8 * TOK, 256), F32),
    ]
    return pl.pallas_call(
        kernel,
        out_shape=(
            jax.ShapeDtypeStruct((TOK, D), BF),
            jax.ShapeDtypeStruct((8 * TOK, 256), BF),
        ),
        in_specs=[anyspace, vmem, vmem, vmem] + [anyspace] * 11,
        out_specs=(vmem, vmem),
        scratch_shapes=[pltpu.VMEM(s, d) for s, d in scratch]
        + [pltpu.SemaphoreType.DMA((N_SEM,))] * 2
        + [pltpu.SemaphoreType.DMA((32,))],
        compiler_params=pltpu.CompilerParams(
            collective_id=0, has_side_effects=True, vmem_limit_bytes=63 * 1024 * 1024
        ),
        name="layer",
    )(
        grad_out,
        expert_ids.T,
        gate_weights.T,
        overflow.T,
        saved_gate[0].transpose(0, 2, 1, 3),
        saved_up[0].transpose(0, 2, 1, 3),
        w_gate[0].T,
        w_up[0].T,
        w_down[0],
        shared_gate_act.T,
        shared_up_act.T,
        ws_gate.T,
        ws_up.T,
        ws_down,
        w_out,
    )


def solution(mesh):
    in_specs = (
        P(("dp", "expert", "tensor"), None),
        P(("dp", "expert", "tensor"), None),
        P(("dp", "expert", "tensor"), None),
        P(("dp", "expert", "tensor"), None),
        P(("expert", "tensor"), None, None, None, "dp"),
        P(("expert", "tensor"), None, None, None, "dp"),
        P(("expert", "tensor"), None, "dp"),
        P(("expert", "tensor"), None, "dp"),
        P(("expert", "tensor"), "dp", None),
        P(("dp", "expert"), "tensor"),
        P(("dp", "expert"), "tensor"),
        P(None, "tensor"),
        P(None, "tensor"),
        P("tensor", None),
        P("tensor", None),
    )
    out_specs = (P(("dp", "expert", "tensor"), None), P(("dp", "expert"), "tensor"))
    return jax.shard_map(body, mesh=mesh, in_specs=in_specs, out_specs=out_specs, check_vma=False)
```

time: 693 us -> 208 us (0.30)
  waiting for transfers between devices: 486 us -> 0 us
  Pallas kernels: 0 us -> 203 us
  local copies, waits for them, and re-layouts: 70.7 us -> 3.75 us
  blocking collectives: 64.6 us -> 0 us
  matrix products: 24 us -> 0 us
  other arithmetic: 16.3 us -> 0 us
  between operations: 14.4 us -> 0.65 us
  starting transfers between devices: 13.4 us -> 0 us
    pallas_call x0 -> x1, Pallas kernels: none -> 203 us  [body(): pl.pallas_call(kernel, out_shape=(jax.ShapeDtypeStruct((TOK, D), BF), jax...]
    psum x1 -> x0, waiting for transfers between devices: 190 us -> none  [body(): lax.psum(partial_value.astype(jnp.bfloat16), 'tensor').astype(jnp.float32)]
    all_gather x4 -> x0, waiting for transfers between devices: 169 us -> none  [the longest x1 81.5 us: body(): lax.all_gather(routed_total, 'tensor', axis=0, tiled=True)]
    reduce_scatter x1 -> x0, waiting for transfers between devices: 74.6 us -> none  [body(): lax.psum_scatter(terms.astype(jnp.bfloat16), 'dp', scatter_dimension=1, t...]
    all_to_all x1 -> x0, blocking collectives: 64.6 us -> none  [body(): lax.all_to_all(filled[:, None], ('expert', 'tensor'), split_axis=0, conca...]
    all_to_all x1 -> x0, waiting for transfers between devices: 50.5 us -> none  [body(): lax.all_to_all(summed[:, 0].astype(jnp.bfloat16), ('expert', 'tensor'), s...]
    convert_element_type x8 -> x0, local copies, waits for them, and re-layouts: 30.2 us -> none  [the longest x3 10 us: swiglu_backward(): up_act.astype(jnp.float32)]
    dot_general x7 -> x0, matrix products: 24 us -> none  [the longest x1 5.14 us: expert_terms(): jnp.einsum('cyg,cog->cyo', capacity_slot_rows, down_projection_weight, pr...]
  transfers between devices with their start and end apart: 7 -> 0, of which waited for: 7 -> 0; matrix products, arithmetic and copies ran while one was open for 12% -> 0% of each run, Pallas kernels for 0% -> 0%
where the time goes in v1:
time: 208 us
  Pallas kernels  203 us (98%)
  local copies, waits for them, and re-layouts  3.75 us (2%)
    pallas_call x1, Pallas kernels, body(): pl.pallas_call(kernel, out_shape=(jax.ShapeDtypeStruct((TOK, D), BF), jax...  203 us

profile of v1, /device:TPU:24, one launch (start us, length us, event | category | flops | bytes accessed | tf_op | source)
XLA Modules:
  0.0 207.5 jit_solution(7299578005336248553)
XLA Ops:
  0.6 203.1 %layer.1 = (bf16[128,2048]{1,0:T(8,128)(2,1)}, bf16[1024,256]{1,0:T(8,128)(2,1)}) custom-call(bf16[128,2048]{1,0:T(8,128)(2,1)} %grad_ref.1, s32[2,128]{1,0:T(2,128)} %bitcast.29, f32[2,128]{1,0:T(2,128)} %bitcast.30, s32[2,128]{1,0:T(2,128)} %bitcast.31, bf16[4,5,64,352]{3,2,1,0:T(8,128)(2,1)} %bitcast.23, bf16[4,5,64,352]{3,2,1,0:T(8,128)(2,1)} %bitcast.24, ...), custom_call_target="tpu_custom_call" | custom-call | tf_op jit(solution)/shard_map/layer/pallas_call | solution.py:449
  203.8 1.9 copy.19
  205.6 1.9 copy.20

commit v2 on v1

--- a/solution.py
+++ b/solution.py
@@ -10,7 +10,7 @@
 MESH = pl.DeviceIdType.MESH
 BF = jnp.bfloat16
 F32 = jnp.float32
-CHUNKS = 2
+CHUNKS = 4
 TOK = 128
 D = 2048
 WIDTH = D // CHUNKS
@@ -20,7 +20,8 @@
 FE = 352
 FS = 176
 DEPTH = 768
-N_SEM = 160
+N_SEM = 200
+HALF = TOK // 2
 
 
 def nn(a, b):
@@ -46,8 +47,8 @@
     grad_ref, ids_ref, gw_ref, ov_ref, sgate_hbm, sup_hbm, wg_hbm, wu_hbm, wd_hbm,
     shg_hbm, shu_hbm, wsg_hbm, wsu_hbm, wsd_hbm, wo_hbm,
     hid_out, ctx_out,
-    G, info, zs, A, Ts, Tr, Us, Ur, V, Z, far_s, near_s, y_s, far_r, near_r, y_r, H,
-    wd, wgu, wsd, wo, sgate, sup, shg, shu, hid, gu, Pm, Wr, Lf, LT, Rk, own, ctx,
+    G, info, zs, A, Ts, Tr, Us, Ur, V, Z, far_s, near_s, y_s, far_r, near_r, y_r, W,
+    wd, wgu, wsd, sgate, sup, shg, shu, hid, gu, Pm, Wr, Lf, LT, Rk, own, ctx, ctx_s, ctx_r,
     ss, rs, ls,
 ):
     dp, z, t = lax.axis_index("dp"), lax.axis_index("expert"), lax.axis_index("tensor")
@@ -97,7 +98,10 @@
         wsd=fetch(wsd_hbm, wsd),
         wg=fetch(wg_hbm, wgu.at[pl.ds(0, FE)]),
         wu=fetch(wu_hbm, wgu.at[pl.ds(384, FE)]),
-        wo=fetch(wo_hbm, wo),
+        wo=fetch(
+            wo_hbm.at[pl.ds(pl.multiple_of(core * TOK, TOK), TOK)],
+            W.at[t, pl.ds(pl.multiple_of(core * TOK, TOK), TOK)],
+        ),
         sgate=fetch(sgate_hbm, sgate),
         sup=fetch(sup_hbm, sup),
         shg=fetch(shg_hbm, shg),
@@ -127,49 +131,49 @@
 
     pl.semaphore_wait(barrier, len(peers))
 
-    def gather0(buf, c):
-        src = buf.at[c, t]
-        return dict(
-            y=send(src, src, across), r=send(src, src, right), l=send(src, src, left)
-        )
-
-    def gather1(buf, c, st):
-        st["y"].wait_recv()
-        src = buf.at[c, x * 2 + yo]
-        st["pr"] = send(src, src, right)
-        st["pl"] = send(src, src, left)
-
-    def forward(buf, c, st, half):
-        a = buf.at[c, xl * 2 + half, pl.ds(0, TOK // 2)]
-        b = buf.at[c, xr * 2 + half, pl.ds(TOK // 2, TOK // 2)]
-        st.setdefault("far", []).extend([send(a, a, right), send(b, b, left)])
-
-    def gather2(buf, c, st):
-        st["r"].wait_recv()
-        st["l"].wait_recv()
-        forward(buf, c, st, yh)
-
-    def gather3(buf, c, st):
-        st["pr"].wait_recv()
-        st["pl"].wait_recv()
-        forward(buf, c, st, yo)
-
-    def gather4(buf, c, st):
-        for cp in st["far"]:
+    def block_of_tokens(c):
+        def view(i, part=None):
+            return G.at[c, i] if part is None else G.at[c, i, pl.ds(part * HALF, HALF)]
+
+        return view
+
+    def block_of_w(i, part=None):
+        if part is None:
+            return W.at[i, pl.ds(pl.multiple_of(core * TOK, TOK), TOK)]
+        return W.at[i, pl.ds(pl.multiple_of(core * TOK + part * HALF, HALF), HALF)]
+
+    def gather_y(view):
+        return dict(view=view, y=send(view(t), view(t), across), far=[])
+
+    def gather_x(g):
+        src = g["view"](t)
+        g["near"] = [send(src, src, right), send(src, src, left)]
+
+    def gather_partner(g):
+        g["y"].wait_recv()
+        src = g["view"](x * 2 + yo)
+        g["partner"] = [send(src, src, right), send(src, src, left)]
+
+    def forward(g, kind, half):
+        for cp in g[kind]:
             cp.wait_recv()
-
-    def gather_all(buf):
-        st = []
-        for c in range(CHUNKS):
-            st.append(gather0(buf, c))
-        return st
-
-    st = []
-    own_in[0].wait()
-    st.append(gather0(G, 0))
-    infos = [send(info.at[t], info.at[t], p) for p in peers[: len(tens)]]
-    for c in range(1, CHUNKS):
+        a = g["view"](xl * 2 + half, 0)
+        b = g["view"](xr * 2 + half, 1)
+        g["far"] += [send(a, a, right), send(b, b, left)]
+
+    def gather_far(g):
+        for cp in g["far"]:
+            cp.wait_recv()
+
+    gs = []
+    for c in range(CHUNKS):
         own_in[c].wait()
+        gs.append(gather_y(block_of_tokens(c)))
+        if c < 2:
+            gather_x(gs[c])
+        if c == 0:
+            infos = [send(info.at[t], info.at[t], p) for p in peers[: len(tens)]]
+    gather_partner(gs[0])
 
     for cp in infos:
         cp.wait_recv()
@@ -200,21 +204,55 @@
             for dz in (1, 7, 2, 6, 3, 5, 4)
         ]
 
-    gather1(G, 0, st[0])
-    gather2(G, 0, st[0])
-    for c in range(1, CHUNKS):
-        st.append(gather0(G, c))
-        gather3(G, c - 1, st[c - 1])
-        gather1(G, c, st[c])
-        gather4(G, c - 1, st[c - 1])
-        if c == 1:
-            zin = []
-        zin.append(dispatch(c - 1))
-        gather2(G, c, st[c])
+    zin, core_in, opp_in = [], [], []
     last = CHUNKS - 1
-    gather3(G, last, st[last])
-    gather4(G, last, st[last])
-    zin.append(dispatch(last))
+
+    def spread(c):
+        for cp in zin[c]:
+            cp.wait_recv()
+        opp_in.append(send(A.at[c, dp], A.at[c, dp], opp))
+        core_in.append([send(A.at[c, dp], A.at[c, dp], sib)])
+
+    def spread_on(c):
+        opp_in[c].wait_recv()
+        core_in[c].append(send(A.at[c, opp_dp], A.at[c, opp_dp], sib))
+
+    def hidden_of(c, d):
+        w = wd[:, c * WIDTH : (c + 1) * WIDTH]
+        h = nt(rows_of(A[c, d]).astype(BF), w)
+        if c == 0:
+            hid[d] = h
+        else:
+            hid[d] = hid[d] + h
+
+    def hidden_all(c):
+        hidden_of(c, dp)
+        hidden_of(c, opp_dp)
+        for cp in core_in[c]:
+            cp.wait_recv()
+        hidden_of(c, sib_dp)
+        hidden_of(c, dia_dp)
+
+    for k in range(CHUNKS):
+        forward(gs[k], "near", yh)
+        if k + 1 < CHUNKS:
+            gather_partner(gs[k + 1])
+        forward(gs[k], "partner", yo)
+        if k + 2 < CHUNKS:
+            gather_x(gs[k + 2])
+        gather_far(gs[k])
+        zin.append(dispatch(k))
+        if k >= 1:
+            spread(k - 1)
+        if k >= 2:
+            spread_on(k - 2)
+        if k == 2:
+            pend["wd"].wait()
+        if k >= 3:
+            hidden_all(k - 3)
+    pend["wo"].wait()
+    gw_ = gather_y(block_of_w)
+    gather_x(gw_)
 
     pend["wsd"].wait()
     pend["shg"].wait()
@@ -229,37 +267,13 @@
     for b in range(8):
         LT[b] = jnp.transpose(Lf[:, b * TOK : (b + 1) * TOK]).astype(BF)
 
-    pend["wd"].wait()
-    core_in, opp_in = [], []
-
-    def spread(c):
-        for cp in zin[c]:
-            cp.wait_recv()
-        opp_in.append(send(A.at[c, dp], A.at[c, dp], opp))
-        core_in.append([send(A.at[c, dp], A.at[c, dp], sib)])
-
-    def spread_on(c):
-        opp_in[c].wait_recv()
-        core_in[c].append(send(A.at[c, opp_dp], A.at[c, opp_dp], sib))
-
-    def hidden_of(c, d):
-        w = wd[:, c * WIDTH : (c + 1) * WIDTH]
-        h = nt(rows_of(A[c, d]).astype(BF), w)
-        if c == 0:
-            hid[d] = h
-        else:
-            hid[d] = hid[d] + h
-
-    spread(0)
-    for c in range(1, CHUNKS):
-        hidden_of(c - 1, dp)
-        spread_on(c - 1)
-        spread(c)
-        hidden_of(c - 1, opp_dp)
-        for cp in core_in[c - 1]:
-            cp.wait_recv()
-        hidden_of(c - 1, sib_dp)
-        hidden_of(c - 1, dia_dp)
+    spread(last)
+    spread_on(last - 1)
+    if last >= 2:
+        hidden_all(last - 2)
+    gather_partner(gw_)
+    forward(gw_, "near", yh)
+    hidden_all(last - 1)
     hidden_of(last, dp)
     spread_on(last)
     pend["sgate"].wait()
@@ -292,6 +306,8 @@
     act(opp_dp)
     act(dp)
 
+    forward(gw_, "partner", yo)
+
     pend["wg"].wait()
     pend["wu"].wait()
 
@@ -302,18 +318,21 @@
         return v.reshape(8, PLANE, WIDTH).astype(BF)
 
     t_in, u_in, z_back = [], [], []
-    for c in range(CHUNKS):
+
+    def sum_core(c):
         Ts[c, 0] = planes(term(c, dia_dp))
         a = send(Ts.at[c, 0], Tr.at[c, 0], sib)
         Ts[c, 1] = planes(term(c, sib_dp))
         b = send(Ts.at[c, 1], Tr.at[c, 1], sib)
         t_in.append((a, b))
-    for c in range(CHUNKS):
+
+    def sum_opp(c):
         v = term(c, opp_dp)
         t_in[c][0].wait_recv()
         Us[c] = planes(v + rows_of(Tr[c, 0]))
         u_in.append(send(Us.at[c], Ur.at[c], opp))
-    for c in range(CHUNKS):
+
+    def sum_dp(c):
         v = term(c, dp)
         t_in[c][1].wait_recv()
         v = v + rows_of(Tr[c, 1])
@@ -324,24 +343,20 @@
             send(V.at[c, (z + dz) % 8], Z.at[c, z], (dp, (z + dz) % 8, t))
             for dz in (1, 7, 2, 6, 3, 5, 4)
         ])
-    for cp in ws_in:
-        cp.wait()
 
     def partial(c, place):
         w = LT[pl.ds(place * 2, 2)].reshape(2 * TOK, DEPTH)
         return nn(w, Rk[c]).reshape(2, TOK, WIDTH)
 
-    half = TOK // 2
     fars, nears, ys = [], [], []
 
     def sum_far(c):
         for cp in z_back[c]:
             cp.wait_recv()
         Rk[c, 0:ROWS] = rows_of(Z[c]).astype(BF)
-        Rk[c, ROWS + 2 * FS : DEPTH] = jnp.zeros((DEPTH - ROWS - 2 * FS, WIDTH), BF)
         v = partial(c, xf).astype(BF)
-        far_s[c, 0] = v[:, 0:half]
-        far_s[c, 1] = v[:, half:TOK]
+        far_s[c, 0] = v[:, 0:HALF]
+        far_s[c, 1] = v[:, HALF:TOK]
         fars.append([
             send(far_s.at[c, 0], far_r.at[c, 0], right),
             send(far_s.at[c, 1], far_r.at[c, 1], left),
@@ -351,54 +366,75 @@
         a = partial(c, xr)
         b = partial(c, xl)
         fars[c][0].wait_recv()
-        near_s[c, 0, :, 0:half] = (a[:, 0:half] + far_r[c, 0].astype(F32)).astype(BF)
-        near_s[c, 0, :, half:TOK] = a[:, half:TOK].astype(BF)
+        near_s[c, 0, :, 0:HALF] = (a[:, 0:HALF] + far_r[c, 0].astype(F32)).astype(BF)
+        near_s[c, 0, :, HALF:TOK] = a[:, HALF:TOK].astype(BF)
         r = send(near_s.at[c, 0], near_r.at[c, 0], right)
         fars[c][1].wait_recv()
-        near_s[c, 1, :, 0:half] = b[:, 0:half].astype(BF)
-        near_s[c, 1, :, half:TOK] = (b[:, half:TOK] + far_r[c, 1].astype(F32)).astype(BF)
+        near_s[c, 1, :, 0:HALF] = b[:, 0:HALF].astype(BF)
+        near_s[c, 1, :, HALF:TOK] = (b[:, HALF:TOK] + far_r[c, 1].astype(F32)).astype(BF)
         l = send(near_s.at[c, 1], near_r.at[c, 1], left)
         nears.append((r, l))
 
     def sum_own(c):
-        own[...] = partial(c, x)
+        mine = own.at[c % 2]
+        mine[...] = partial(c, x)
         nears[c][0].wait_recv()
         nears[c][1].wait_recv()
         y_s[c] = (
-            own[yo] + near_r[c, 0, yo].astype(F32) + near_r[c, 1, yo].astype(F32)
+            mine[yo] + near_r[c, 0, yo].astype(F32) + near_r[c, 1, yo].astype(F32)
         ).astype(BF)
         ys.append(send(y_s.at[c], y_r.at[c], across))
-        own[yh] = own[yh] + near_r[c, 0, yh].astype(F32) + near_r[c, 1, yh].astype(F32)
+        mine[yh] = mine[yh] + near_r[c, 0, yh].astype(F32) + near_r[c, 1, yh].astype(F32)
 
     def finish(c):
+        cols = slice(c * WIDTH, (c + 1) * WIDTH)
         ys[c].wait_recv()
-        v = (own[yh] + y_r[c].astype(F32) + G[c, t].astype(F32)).astype(BF)
-        H[c, t] = v
-        hid_out[:, c * WIDTH : (c + 1) * WIDTH] = v
-
-    hs = []
-    sum_far(0)
-    for c in range(CHUNKS):
-        sum_near(c)
-        if c + 1 < CHUNKS:
-            sum_far(c + 1)
-        sum_own(c)
-        finish(c)
-        hs.append(gather0(H, c))
-    for c in range(CHUNKS):
-        gather1(H, c, hs[c])
-        gather2(H, c, hs[c])
-    pend["wo"].wait()
-    for c in range(CHUNKS):
-        gather3(H, c, hs[c])
-    for c in range(CHUNKS):
-        gather4(H, c, hs[c])
-        v = nt(H[c].reshape(8 * TOK, WIDTH), wo[:, c * WIDTH : (c + 1) * WIDTH])
+        v = (own[c % 2, yh] + y_r[c].astype(F32) + G[c, t].astype(F32)).astype(BF)
+        hid_out[:, cols] = v
+        w = nt(v, W[:, :, cols].reshape(D, WIDTH))
         if c == 0:
-            ctx[...] = v
+            ctx[...] = w
         else:
-            ctx[...] = ctx[...] + v
-    ctx_out[...] = ctx[...].astype(BF)
+            ctx[...] = ctx[...] + w
+
+    sum_core(0)
+    for k in range(CHUNKS + 5):
+        if k + 1 < CHUNKS:
+            sum_core(k + 1)
+        if k == CHUNKS - 1:
+            gather_far(gw_)
+            mine = W.at[:, pl.ds(pl.multiple_of(core * TOK, TOK), TOK)]
+            w_in = send(mine, mine, sib)
+        if k < CHUNKS:
+            sum_opp(k)
+        if 0 <= k - 1 < CHUNKS:
+            sum_dp(k - 1)
+        if k == 1:
+            for cp in ws_in:
+                cp.wait()
+            for c in range(CHUNKS):
+                Rk[c, ROWS + 2 * FS : DEPTH] = jnp.zeros((DEPTH - ROWS - 2 * FS, WIDTH), BF)
+        if k == CHUNKS:
+            pass
+        if 0 <= k - 2 < CHUNKS:
+            sum_far(k - 2)
+        if 0 <= k - 3 < CHUNKS:
+            sum_near(k - 3)
+        if k == CHUNKS:
+            w_in.wait_recv()
+        if 0 <= k - 5 < CHUNKS:
+            finish(k - 5)
+        if 0 <= k - 4 < CHUNKS:
+            sum_own(k - 4)
+    for b in range(8):
+        ctx_s[b] = ctx[:, b * 256 : (b + 1) * 256].astype(BF)
+    outs = [
+        send(ctx_s.at[p[2]], ctx_r.at[t], p) for p in peers[: len(tens)]
+    ]
+    ctx_r[t] = ctx_s[t]
+    for cp in outs:
+        cp.wait_recv()
+    ctx_out[...] = ctx_r[...].reshape(8 * TOK, 256)
     for cp in sent:
         cp.wait_send()
 
@@ -427,11 +463,10 @@
         ((C, 2, 2, TOK // 2, W), BF),
         ((C, 2, 2, TOK, W), BF),
         ((C, TOK, W), BF),
-        ((C, 8, TOK, W), BF),
+        ((8, 256, D), BF),
         ((FE, D), BF),
         ((DEPTH, D), BF),
         ((FS, D), BF),
-        ((256, D), BF),
         ((4, CAP, 64, FE), BF),
         ((4, CAP, 64, FE), BF),
         ((FS, 8 * TOK), BF),
@@ -443,8 +478,10 @@
         ((DEPTH, 8 * TOK), F32),
         ((8, TOK, DEPTH), BF),
         ((C, DEPTH, W), BF),
-        ((2, TOK, W), F32),
-        ((8 * TOK, 256), F32),
+        ((2, 2, TOK, W), F32),
+        ((TOK, D), F32),
+        ((8, TOK, 256), BF),
+        ((8, TOK, 256), BF),
     ]
     return pl.pallas_call(
         kernel,

time: 208 us -> 173 us (0.83)
  Pallas kernels: 203 us -> 169 us
    pallas_call x1, Pallas kernels: 203 us -> 169 us  [body(): pl.pallas_call(kernel, out_shape=(jax.ShapeDtypeStruct((TOK, D), BF), jax...]
where the time goes in v2:
time: 173 us
  Pallas kernels  169 us (98%)
  local copies, waits for them, and re-layouts  3.75 us (2%)
    pallas_call x1, Pallas kernels, body(): pl.pallas_call(kernel, out_shape=(jax.ShapeDtypeStruct((TOK, D), BF), jax...  169 us
    unnamed x2, local copies, waits for them, and re-layouts  3.75 us

profile of v2, /device:TPU:24, one launch (start us, length us, event | category | flops | bytes accessed | tf_op | source)
XLA Modules:
  0.0 173.3 jit_solution(2433814210639946023)
XLA Ops:
  0.6 168.9 %layer.1 = (bf16[128,2048]{1,0:T(8,128)(2,1)}, bf16[1024,256]{1,0:T(8,128)(2,1)}) custom-call(bf16[128,2048]{1,0:T(8,128)(2,1)} %grad_ref.1, s32[2,128]{1,0:T(2,128)} %bitcast.29, f32[2,128]{1,0:T(2,128)} %bitcast.30, s32[2,128]{1,0:T(2,128)} %bitcast.31, bf16[4,5,64,352]{3,2,1,0:T(8,128)(2,1)} %bitcast.23, bf16[4,5,64,352]{3,2,1,0:T(8,128)(2,1)} %bitcast.24, ...), custom_call_target="tpu_custom_call" | custom-call | tf_op jit(solution)/shard_map/layer/pallas_call | solution.py:486
  169.5 1.9 %copy.19 = bf16[128,2048]{1,0:T(8,128)(2,1)} copy(bf16[128,2048]{1,0:T(8,128)(2,1)} %get-tuple-element.4) | data formatting | bytes 1048576
  171.4 1.9 %copy.20 = bf16[1024,256]{1,0:T(8,128)(2,1)} copy(bf16[1024,256]{1,0:T(8,128)(2,1)} %get-tuple-element.5) | data formatting | bytes 1048576

commit v3 on v2

--- a/solution.py
+++ b/solution.py
@@ -20,7 +20,7 @@
 FE = 352
 FS = 176
 DEPTH = 768
-N_SEM = 200
+N_SEM = 260
 HALF = TOK // 2
 
 
@@ -48,7 +48,7 @@
     shg_hbm, shu_hbm, wsg_hbm, wsu_hbm, wsd_hbm, wo_hbm,
     hid_out, ctx_out,
     G, info, zs, A, Ts, Tr, Us, Ur, V, Z, far_s, near_s, y_s, far_r, near_r, y_r, W,
-    wd, wgu, wsd, sgate, sup, shg, shu, hid, gu, Pm, Wr, Lf, LT, Rk, own, ctx, ctx_s, ctx_r,
+    wd, wgu, wsd, sgate, sup, shg, shu, hid, gu, Xs, Xr, Q, Lf, LT, Rk, own, ctx, ctx_s, ctx_r,
     ss, rs, ls,
 ):
     dp, z, t = lax.axis_index("dp"), lax.axis_index("expert"), lax.axis_index("tensor")
@@ -129,6 +129,24 @@
         [ids.astype(F32), slots[0], slots[1], routed_weight, shared_weight, shared_weight], axis=0
     )
 
+    row_ids = lax.broadcasted_iota(jnp.int32, (ROWS, TOK), 0)
+    weight = jnp.zeros((ROWS, 1), F32)
+    pick = jnp.zeros((ROWS, TOK), F32)
+    for k in range(2):
+        e = ids[k : k + 1, :]
+        code = (e % 8) * PLANE + (e // 8) * CAP + slots[k].astype(jnp.int32)
+        on = (row_ids == code).astype(F32)
+        weight = weight + jnp.sum(on * routed_weight[k : k + 1, :], axis=1, keepdims=True)
+        pick = pick + on
+    pick = pick.astype(BF)
+    r = lax.broadcasted_iota(jnp.int32, (ROWS, ROWS), 0)
+    from_row = (r % 8) * PLANE + (r // PLANE) * CAP + (r % PLANE) // 8
+    Q[...] = (lax.broadcasted_iota(jnp.int32, (ROWS, ROWS), 1) == from_row).astype(F32).astype(BF)
+    for c in range(CHUNKS):
+        own_in[c].wait()
+        Xs[c] = (nn(pick, G[c, t]) * weight).reshape(8, PLANE, WIDTH).astype(BF)
+        Xr[c, t] = Xs[c, t]
+
     pl.semaphore_wait(barrier, len(peers))
 
     def block_of_tokens(c):
@@ -165,39 +183,18 @@
         for cp in g["far"]:
             cp.wait_recv()
 
-    gs = []
+    x_in = []
     for c in range(CHUNKS):
-        own_in[c].wait()
-        gs.append(gather_y(block_of_tokens(c)))
-        if c < 2:
-            gather_x(gs[c])
-        if c == 0:
+        x_in.append([send(Xs.at[c, p[2]], Xr.at[c, t], p) for p in peers[: len(tens)]])
+        if c == 1:
             infos = [send(info.at[t], info.at[t], p) for p in peers[: len(tens)]]
-    gather_partner(gs[0])
-
-    for cp in infos:
-        cp.wait_recv()
-    row_ids = lax.broadcasted_iota(jnp.int32, (ROWS, TOK), 0)
-    weight = jnp.zeros((ROWS, 1), F32)
-    Lf[...] = jnp.zeros_like(Lf)
-    for b in range(8):
-        part = info[b]
-        hit = []
-        for k in range(2):
-            e = part[k : k + 1, :].astype(jnp.int32)
-            j = part[2 + k : 3 + k, :].astype(jnp.int32)
-            code = jnp.where(e % 8 == t, (e // 8) * PLANE + j * 8 + b, -1)
-            on = (row_ids == code).astype(F32)
-            weight = weight + jnp.sum(on * part[4 + k : 5 + k, :], axis=1, keepdims=True)
-            hit.append(on)
-        both = hit[0] + hit[1]
-        Lf[0:ROWS, b * TOK : (b + 1) * TOK] = both
-        Pm[:, b * TOK : (b + 1) * TOK] = both.astype(BF)
-    Wr[...] = jnp.broadcast_to(weight, Wr.shape)
+    gs = [gather_y(block_of_tokens(c)) for c in range(CHUNKS)]
+    gather_x(gs[0])
 
     def dispatch(c):
-        got = nn(Pm[...], G[c].reshape(8 * TOK, WIDTH)) * Wr[:, 0:1]
-        zs[c] = got.reshape(8, PLANE, WIDTH).astype(BF)
+        for cp in x_in[c]:
+            cp.wait_recv()
+        zs[c] = nn(Q[...], rows_of(Xr[c]).astype(BF)).reshape(8, PLANE, WIDTH).astype(BF)
         A[c, dp, z] = zs[c, z]
         return [
             send(zs.at[c, (z + dz) % 8], A.at[c, dp, z], (dp, (z + dz) % 8, t))
@@ -232,52 +229,6 @@
             cp.wait_recv()
         hidden_of(c, sib_dp)
         hidden_of(c, dia_dp)
-
-    for k in range(CHUNKS):
-        forward(gs[k], "near", yh)
-        if k + 1 < CHUNKS:
-            gather_partner(gs[k + 1])
-        forward(gs[k], "partner", yo)
-        if k + 2 < CHUNKS:
-            gather_x(gs[k + 2])
-        gather_far(gs[k])
-        zin.append(dispatch(k))
-        if k >= 1:
-            spread(k - 1)
-        if k >= 2:
-            spread_on(k - 2)
-        if k == 2:
-            pend["wd"].wait()
-        if k >= 3:
-            hidden_all(k - 3)
-    pend["wo"].wait()
-    gw_ = gather_y(block_of_w)
-    gather_x(gw_)
-
-    pend["wsd"].wait()
-    pend["shg"].wait()
-    pend["shu"].wait()
-    sw = jnp.concatenate([info[b, 6:7, :] for b in range(8)], axis=1)
-    sh = jnp.zeros((FS, 8 * TOK), F32)
-    for c in range(CHUNKS):
-        sh = sh + nt(wsd[:, c * WIDTH : (c + 1) * WIDTH], G[c].reshape(8 * TOK, WIDTH))
-    sg, su = swiglu_backward(sh * sw, shg[...].astype(F32), shu[...].astype(F32))
-    Lf[ROWS : ROWS + FS, :] = sg
-    Lf[ROWS + FS : ROWS + 2 * FS, :] = su
-    for b in range(8):
-        LT[b] = jnp.transpose(Lf[:, b * TOK : (b + 1) * TOK]).astype(BF)
-
-    spread(last)
-    spread_on(last - 1)
-    if last >= 2:
-        hidden_all(last - 2)
-    gather_partner(gw_)
-    forward(gw_, "near", yh)
-    hidden_all(last - 1)
-    hidden_of(last, dp)
-    spread_on(last)
-    pend["sgate"].wait()
-    pend["sup"].wait()
 
     def act(d):
         h4 = hid[d].reshape(8, CAP, 8, FE)
@@ -293,23 +244,82 @@
         gu[d, :, 0:FE] = jnp.stack(gs, axis=1).reshape(ROWS, FE).astype(BF)
         gu[d, :, 384 : 384 + FE] = jnp.stack(us, axis=1).reshape(ROWS, FE).astype(BF)
 
-    gu[...] = jnp.zeros_like(gu)
+    def shared_units():
+        for cp in infos:
+            cp.wait_recv()
+        row_ids = lax.broadcasted_iota(jnp.int32, (ROWS, TOK), 0)
+        Lf[ROWS + 2 * FS : DEPTH, :] = jnp.zeros((DEPTH - ROWS - 2 * FS, 8 * TOK), F32)
+        for b in range(8):
+            part = info[b]
+            hit = []
+            for k in range(2):
+                e = part[k : k + 1, :].astype(jnp.int32)
+                j = part[2 + k : 3 + k, :].astype(jnp.int32)
+                code = jnp.where(e % 8 == t, (e // 8) * PLANE + j * 8 + b, -1)
+                on = (row_ids == code).astype(F32)
+                hit.append(on)
+            Lf[0:ROWS, b * TOK : (b + 1) * TOK] = hit[0] + hit[1]
+
+        for g in gs:
+            gather_far(g)
+        pend["wsd"].wait()
+        pend["shg"].wait()
+        pend["shu"].wait()
+        sw = jnp.concatenate([info[b, 6:7, :] for b in range(8)], axis=1)
+        sh = jnp.zeros((FS, 8 * TOK), F32)
+        for c in range(CHUNKS):
+            sh = sh + nt(wsd[:, c * WIDTH : (c + 1) * WIDTH], G[c].reshape(8 * TOK, WIDTH))
+        sg, su = swiglu_backward(sh * sw, shg[...].astype(F32), shu[...].astype(F32))
+        Lf[ROWS : ROWS + FS, :] = sg
+        Lf[ROWS + FS : ROWS + 2 * FS, :] = su
+        for b in range(8):
+            LT[b] = jnp.transpose(Lf[:, b * TOK : (b + 1) * TOK]).astype(BF)
+
+
+    for k in range(CHUNKS):
+        zin.append(dispatch(k))
+        if k >= 1:
+            spread(k - 1)
+            gather_partner(gs[k - 1])
+            forward(gs[k - 1], "near", yh)
+            gather_x(gs[k])
+        if k == 2:
+            pend["wd"].wait()
+        if k >= 2:
+            spread_on(k - 2)
+            forward(gs[k - 2], "partner", yo)
+        if k >= 3:
+            hidden_all(k - 3)
+    gu[:, :, FE:384] = jnp.zeros((4, ROWS, 384 - FE), BF)
+    gu[:, :, 384 + FE : DEPTH] = jnp.zeros((4, ROWS, DEPTH - 384 - FE), BF)
+    pend["wg"].wait()
+    pend["wu"].wait()
     wgu[FE:384, :] = jnp.zeros((384 - FE, D), BF)
     wgu[384 + FE : DEPTH, :] = jnp.zeros((DEPTH - 384 - FE, D), BF)
-    hidden_of(last, opp_dp)
+    pend["sgate"].wait()
+    pend["sup"].wait()
+    spread(last)
+    gather_partner(gs[last])
+    forward(gs[last], "near", yh)
+    spread_on(last - 1)
+    forward(gs[last - 1], "partner", yo)
+    hidden_all(last - 2)
+    hidden_all(last - 1)
+    hidden_of(last, dp)
+    act(dp)
+    spread_on(last)
+    forward(gs[last], "partner", yo)
+    pend["wo"].wait()
+    gw_ = gather_y(block_of_w)
+    gather_x(gw_)
     core_in[last][0].wait_recv()
     hidden_of(last, sib_dp)
     act(sib_dp)
+    hidden_of(last, opp_dp)
+    act(opp_dp)
     core_in[last][1].wait_recv()
     hidden_of(last, dia_dp)
     act(dia_dp)
-    act(opp_dp)
-    act(dp)
-
-    forward(gw_, "partner", yo)
-
-    pend["wg"].wait()
-    pend["wu"].wait()
 
     def term(c, d):
         return nn(gu[d], wgu[:, c * WIDTH : (c + 1) * WIDTH])
@@ -401,7 +411,12 @@
     for k in range(CHUNKS + 5):
         if k + 1 < CHUNKS:
             sum_core(k + 1)
-        if k == CHUNKS - 1:
+        if k == 0:
+            gather_partner(gw_)
+            forward(gw_, "near", yh)
+        if k == 2:
+            forward(gw_, "partner", yo)
+        if k == CHUNKS:
             gather_far(gw_)
             mine = W.at[:, pl.ds(pl.multiple_of(core * TOK, TOK), TOK)]
             w_in = send(mine, mine, sib)
@@ -410,17 +425,16 @@
         if 0 <= k - 1 < CHUNKS:
             sum_dp(k - 1)
         if k == 1:
+            shared_units()
             for cp in ws_in:
                 cp.wait()
             for c in range(CHUNKS):
                 Rk[c, ROWS + 2 * FS : DEPTH] = jnp.zeros((DEPTH - ROWS - 2 * FS, WIDTH), BF)
-        if k == CHUNKS:
-            pass
         if 0 <= k - 2 < CHUNKS:
             sum_far(k - 2)
         if 0 <= k - 3 < CHUNKS:
             sum_near(k - 3)
-        if k == CHUNKS:
+        if k == CHUNKS + 1:
             w_in.wait_recv()
         if 0 <= k - 5 < CHUNKS:
             finish(k - 5)
@@ -473,8 +487,9 @@
         ((FS, 8 * TOK), BF),
         ((4, ROWS, FE), F32),
         ((4, ROWS, DEPTH), BF),
-        ((ROWS, 8 * TOK), BF),
-        ((ROWS, TOK), F32),
+        ((C, 8, PLANE, W), BF),
+        ((C, 8, PLANE, W), BF),
+        ((ROWS, ROWS), BF),
         ((DEPTH, 8 * TOK), F32),
         ((8, TOK, DEPTH), BF),
         ((C, DEPTH, W), BF),

time: 173 us -> 166 us (0.960)
  Pallas kernels: 169 us -> 160 us
    pallas_call x1, Pallas kernels: 169 us -> 160 us  [body(): pl.pallas_call(kernel, out_shape=(jax.ShapeDtypeStruct((TOK, D), BF), jax...]
where the time goes in v3:
time: 166 us; the launch traced here: 165 us
  Pallas kernels  160 us (96%)
  local copies, waits for them, and re-layouts  3.75 us (2%)
    pallas_call x1, Pallas kernels, body(): pl.pallas_call(kernel, out_shape=(jax.ShapeDtypeStruct((TOK, D), BF), jax...  160 us
    unnamed x2, local copies, waits for them, and re-layouts  3.75 us

profile of v3, /device:TPU:24, one launch (start us, length us, event | category | flops | bytes accessed | tf_op | source)
XLA Modules:
  0.0 164.8 jit_solution(8012731170304348573)
XLA Ops:
  0.6 160.4 %layer.1 = (bf16[128,2048]{1,0:T(8,128)(2,1)}, bf16[1024,256]{1,0:T(8,128)(2,1)}) custom-call(bf16[128,2048]{1,0:T(8,128)(2,1)} %grad_ref.1, s32[2,128]{1,0:T(2,128)} %bitcast.29, f32[2,128]{1,0:T(2,128)} %bitcast.30, s32[2,128]{1,0:T(2,128)} %bitcast.31, bf16[4,5,64,352]{3,2,1,0:T(8,128)(2,1)} %bitcast.23, bf16[4,5,64,352]{3,2,1,0:T(8,128)(2,1)} %bitcast.24, ...), custom_call_target="tpu_custom_call" | custom-call | tf_op jit(solution)/shard_map/layer/pallas_call | solution.py:501
  161.0 1.9 %copy.19 = bf16[128,2048]{1,0:T(8,128)(2,1)} copy(bf16[128,2048]{1,0:T(8,128)(2,1)} %get-tuple-element.4) | data formatting | bytes 1048576
  162.9 1.9 %copy.20 = bf16[1024,256]{1,0:T(8,128)(2,1)} copy(bf16[1024,256]{1,0:T(8,128)(2,1)} %get-tuple-element.5) | data formatting | bytes 1048576

commit v4 on v3

--- a/solution.py
+++ b/solution.py
@@ -142,11 +142,13 @@
     r = lax.broadcasted_iota(jnp.int32, (ROWS, ROWS), 0)
     from_row = (r % 8) * PLANE + (r // PLANE) * CAP + (r % PLANE) // 8
     Q[...] = (lax.broadcasted_iota(jnp.int32, (ROWS, ROWS), 1) == from_row).astype(F32).astype(BF)
-    for c in range(CHUNKS):
+
+    def pick_rows(c):
         own_in[c].wait()
         Xs[c] = (nn(pick, G[c, t]) * weight).reshape(8, PLANE, WIDTH).astype(BF)
         Xr[c, t] = Xs[c, t]
 
+    pick_rows(0)
     pl.semaphore_wait(barrier, len(peers))
 
     def block_of_tokens(c):
@@ -185,6 +187,8 @@
 
     x_in = []
     for c in range(CHUNKS):
+        if c:
+            pick_rows(c)
         x_in.append([send(Xs.at[c, p[2]], Xr.at[c, t], p) for p in peers[: len(tens)]])
         if c == 1:
             infos = [send(info.at[t], info.at[t], p) for p in peers[: len(tens)]]
@@ -301,6 +305,9 @@
     spread(last)
     gather_partner(gs[last])
     forward(gs[last], "near", yh)
+    pend["wo"].wait()
+    gw_ = dict(view=block_of_w, far=[])
+    gather_x(gw_)
     spread_on(last - 1)
     forward(gs[last - 1], "partner", yo)
     hidden_all(last - 2)
@@ -309,9 +316,7 @@
     act(dp)
     spread_on(last)
     forward(gs[last], "partner", yo)
-    pend["wo"].wait()
-    gw_ = gather_y(block_of_w)
-    gather_x(gw_)
+    gw_["y"] = gather_y(block_of_w)["y"]
     core_in[last][0].wait_recv()
     hidden_of(last, sib_dp)
     act(sib_dp)
@@ -401,7 +406,10 @@
         ys[c].wait_recv()
         v = (own[c % 2, yh] + y_r[c].astype(F32) + G[c, t].astype(F32)).astype(BF)
         hid_out[:, cols] = v
-        w = nt(v, W[:, :, cols].reshape(D, WIDTH))
+
+    def project(c):
+        cols = slice(c * WIDTH, (c + 1) * WIDTH)
+        w = nt(hid_out[:, cols], W[:, :, cols].reshape(D, WIDTH))
         if c == 0:
             ctx[...] = w
         else:
@@ -411,20 +419,16 @@
     for k in range(CHUNKS + 5):
         if k + 1 < CHUNKS:
             sum_core(k + 1)
+        if k < CHUNKS:
+            sum_opp(k)
         if k == 0:
             gather_partner(gw_)
             forward(gw_, "near", yh)
         if k == 2:
             forward(gw_, "partner", yo)
-        if k == CHUNKS:
-            gather_far(gw_)
-            mine = W.at[:, pl.ds(pl.multiple_of(core * TOK, TOK), TOK)]
-            w_in = send(mine, mine, sib)
-        if k < CHUNKS:
-            sum_opp(k)
         if 0 <= k - 1 < CHUNKS:
             sum_dp(k - 1)
-        if k == 1:
+        if k == 2:
             shared_units()
             for cp in ws_in:
                 cp.wait()
@@ -434,12 +438,20 @@
             sum_far(k - 2)
         if 0 <= k - 3 < CHUNKS:
             sum_near(k - 3)
-        if k == CHUNKS + 1:
-            w_in.wait_recv()
+        if k == CHUNKS:
+            gather_far(gw_)
+            mine = W.at[:, pl.ds(pl.multiple_of(core * TOK, TOK), TOK)]
+            w_in = send(mine, mine, sib)
         if 0 <= k - 5 < CHUNKS:
             finish(k - 5)
         if 0 <= k - 4 < CHUNKS:
             sum_own(k - 4)
+        if k == CHUNKS + 2:
+            w_in.wait_recv()
+        if 0 <= k - 6 < CHUNKS:
+            project(k - 6)
+    for c in range(CHUNKS - 1, CHUNKS):
+        project(c)
     for b in range(8):
         ctx_s[b] = ctx[:, b * 256 : (b + 1) * 256].astype(BF)
     outs = [
@@ -498,12 +510,13 @@
         ((8, TOK, 256), BF),
         ((8, TOK, 256), BF),
     ]
-    return pl.pallas_call(
+    shapes = (
+        jax.ShapeDtypeStruct((TOK, D), BF),
+        jax.ShapeDtypeStruct((8 * TOK, 256), BF),
+    )
+    made = pl.pallas_call(
         kernel,
-        out_shape=(
-            jax.ShapeDtypeStruct((TOK, D), BF),
-            jax.ShapeDtypeStruct((8 * TOK, 256), BF),
-        ),
+        out_shape=shapes,
         in_specs=[anyspace, vmem, vmem, vmem] + [anyspace] * 11,
         out_specs=(vmem, vmem),
         scratch_shapes=[pltpu.VMEM(s, d) for s, d in scratch]
@@ -530,6 +543,7 @@
         ws_down,
         w_out,
     )
+    return made
 
 
 def solution(mesh):

time: 166 us -> 165 us (level)
  no operation moved by 1% of the time
where the time goes in v4:
time: 165 us; the launch traced here: 164 us
  Pallas kernels  159 us (96%)
  local copies, waits for them, and re-layouts  3.75 us (2%)
    pallas_call x1, Pallas kernels, body(): pl.pallas_call(kernel, out_shape=shapes, in_specs=[anyspace, vmem, vmem,...  159 us
    unnamed x2, local copies, waits for them, and re-layouts  3.75 us

profile of v4, /device:TPU:24, one launch (start us, length us, event | category | flops | bytes accessed | tf_op | source)
XLA Modules:
  0.0 163.9 jit_solution(11429735604229678109)
XLA Ops:
  0.6 159.5 %layer.1 = (bf16[128,2048]{1,0:T(8,128)(2,1)}, bf16[1024,256]{1,0:T(8,128)(2,1)}) custom-call(bf16[128,2048]{1,0:T(8,128)(2,1)} %grad_ref.1, s32[2,128]{1,0:T(2,128)} %bitcast.29, f32[2,128]{1,0:T(2,128)} %bitcast.30, s32[2,128]{1,0:T(2,128)} %bitcast.31, bf16[4,5,64,352]{3,2,1,0:T(8,128)(2,1)} %bitcast.23, bf16[4,5,64,352]{3,2,1,0:T(8,128)(2,1)} %bitcast.24, ...), custom_call_target="tpu_custom_call" | custom-call | tf_op jit(solution)/shard_map/layer/pallas_call | solution.py:517
  160.1 1.9 %copy.19 = bf16[128,2048]{1,0:T(8,128)(2,1)} copy(bf16[128,2048]{1,0:T(8,128)(2,1)} %get-tuple-element.4) | data formatting | bytes 1048576
  162.0 1.9 %copy.20 = bf16[1024,256]{1,0:T(8,128)(2,1)} copy(bf16[1024,256]{1,0:T(8,128)(2,1)} %get-tuple-element.5) | data formatting | bytes 1048576
